TPU v7x, 512 devices: a whole 4x8x8 slice. The times are simulated.
512 devices in a mesh: seg: 64 (over y, x, core), tp: 8 (over z).
Axes of the slice: x: 4, y: 8, z: 8, core: 2. Of those that a mesh axis runs over, the one named last changes fastest.
Arguments:
- queries: bfloat16 [16384, 8192], P('seg', 'tp'), may hold values from -260 to 260
- key_rows: bfloat16 [16384, 1024], P('seg', 'tp'), may hold values from -4 to 4
- value_rows: bfloat16 [16384, 1024], P('seg', 'tp'), may hold values from -6 to 6
- grad_out: bfloat16 [16384, 8192], P('seg', 'tp'), may hold values from -6 to 6
- seg_order: int32 [64], replicated, may hold values from 0 to 63, each once
Outputs:
- grad_queries: bfloat16 [16384, 8192], P(('seg', 'tp'))
- grad_keys: bfloat16 [16384, 1024], P(('seg', 'tp'))
- grad_values: bfloat16 [16384, 1024], P(('seg', 'tp'))
Inputs may be any that keep to these rules, and one draw needn't show every extreme that they name: `seg_order`: each position 0 to 63 once.
All inputs are finite; a program needn't handle non-finite values.
Results may differ from a plain program's by a relative error of at most 0.0065.
Values may be sent and summed in bfloat16 or wider, within the bound.
A program may use at most 64 MiB of HBM per device.

v0:
```python
import jax
import jax.numpy as jnp
from jax import lax
from jax.sharding import PartitionSpec as P

HEAD_DIM = 128
SUMM = 32


def local(queries, key_rows, value_rows, grad_out, seg_order):
    seg_len = queries.shape[0]
    kv_count = key_rows.shape[1] // HEAD_DIM
    group = queries.shape[1] // key_rows.shape[1]
    scaling = HEAD_DIM ** (-0.5)
    prior_k, prior_v = (
        lax.all_gather(key_rows[seg_len - SUMM :], "seg", axis=0, tiled=True),
        lax.all_gather(value_rows[seg_len - SUMM :], "seg", axis=0, tiled=True),
    )
    prior_rows = prior_k.shape[0]
    all_k = jnp.concatenate([key_rows, prior_k], 0)
    all_v = jnp.concatenate([value_rows, prior_v], 0)
    width = all_k.shape[0]
    own_order = seg_order[lax.axis_index("seg")]
    slot_order = jnp.repeat(seg_order, SUMM)
    row_pos = lax.broadcasted_iota(jnp.int32, (seg_len, seg_len), 0)
    col_pos = lax.broadcasted_iota(jnp.int32, (seg_len, seg_len), 1)
    prior_ok = jnp.broadcast_to((slot_order < own_order)[None, :], (seg_len, prior_rows))
    visible = jnp.concatenate([col_pos <= row_pos, prior_ok], 1)
    visible = jnp.concatenate([visible, visible], 0)
    q_four = queries.reshape(seg_len, kv_count, group, HEAD_DIM)
    g_four = grad_out.reshape(seg_len, kv_count, group, HEAD_DIM)
    contract_last = (((1,), (1,)), ((), ()))
    contract_first = (((0,), (0,)), ((), ()))
    head_k = all_k
    head_v = all_v
    q_pairs = q_four[:, 0].transpose(1, 0, 2).reshape(group // 2, 2 * seg_len, HEAD_DIM)
    g_pairs = g_four[:, 0].transpose(1, 0, 2).reshape(group // 2, 2 * seg_len, HEAD_DIM)

    def head_step(carry, pair, head_k=head_k, head_v=head_v):
        q_rows, g_rows = pair
        scores = (
            lax.dot_general(q_rows, head_k, contract_last, preferred_element_type=jnp.float32)
            * scaling
        )
        scores = jnp.where(visible, scores, -jnp.inf)
        top = jnp.max(scores, 1, keepdims=True)
        weights = jnp.exp(scores - top)
        probs = weights / jnp.sum(weights, 1, keepdims=True)
        grad_probs = lax.dot_general(
            g_rows, head_v, contract_last, preferred_element_type=jnp.float32
        )
        delta_rows = jnp.sum(probs * grad_probs, 1, keepdims=True)
        grad_scores = (probs * (grad_probs - delta_rows)).astype(jnp.bfloat16)
        probs_low = probs.astype(jnp.bfloat16)
        value_term = lax.dot_general(
            probs_low, g_rows, contract_first, preferred_element_type=jnp.float32
        )
        key_term = (
            lax.dot_general(grad_scores, q_rows, contract_first, preferred_element_type=jnp.float32)
            * scaling
        )
        dq_rows = (
            jnp.dot(grad_scores, head_k, preferred_element_type=jnp.float32) * scaling
        ).astype(jnp.bfloat16)
        return ((carry[0] + key_term, carry[1] + value_term), dq_rows)

    zeros = jnp.zeros((width, HEAD_DIM), jnp.float32)
    (dk_head, dv_head), dq_head = lax.scan(head_step, (zeros, zeros), (q_pairs, g_pairs))
    dq_parts = [dq_head.reshape(group, seg_len, HEAD_DIM)]
    dk_parts = [dk_head]
    dv_parts = [dv_head]
    dq_all = jnp.stack(dq_parts).transpose(2, 0, 1, 3).reshape(seg_len, kv_count * group * HEAD_DIM)
    dk_stack = jnp.stack(dk_parts)
    dv_stack = jnp.stack(dv_parts)
    local_dk = dk_stack[:, :seg_len].transpose(1, 0, 2).reshape(seg_len, kv_count * HEAD_DIM)
    local_dv = dv_stack[:, :seg_len].transpose(1, 0, 2).reshape(seg_len, kv_count * HEAD_DIM)
    prior_dk = dk_stack[:, seg_len:].transpose(1, 0, 2).reshape(prior_rows, kv_count * HEAD_DIM)
    prior_dv = dv_stack[:, seg_len:].transpose(1, 0, 2).reshape(prior_rows, kv_count * HEAD_DIM)
    slots = prior_rows // SUMM
    back_k, back_v = (
        lax.all_to_all(
            prior_dk.reshape(slots, SUMM, kv_count * HEAD_DIM),
            "seg",
            split_axis=0,
            concat_axis=0,
            tiled=True,
        ),
        lax.all_to_all(
            prior_dv.reshape(slots, SUMM, kv_count * HEAD_DIM),
            "seg",
            split_axis=0,
            concat_axis=0,
            tiled=True,
        ),
    )
    back_k = jnp.sum(back_k, 0)
    back_v = jnp.sum(back_v, 0)
    local_dk = local_dk.at[seg_len - SUMM :].add(back_k).astype(jnp.bfloat16)
    local_dv = local_dv.at[seg_len - SUMM :].add(back_v).astype(jnp.bfloat16)
    grad_queries, grad_keys, grad_values = (
        lax.all_to_all(dq_all, "tp", split_axis=0, concat_axis=1, tiled=True),
        lax.all_to_all(local_dk, "tp", split_axis=0, concat_axis=1, tiled=True),
        lax.all_to_all(local_dv, "tp", split_axis=0, concat_axis=1, tiled=True),
    )
    return (grad_queries, grad_keys, grad_values)


def solution(mesh):
    in_specs = (P("seg", "tp"), P("seg", "tp"), P("seg", "tp"), P("seg", "tp"), P())
    out_specs = (P(("seg", "tp"), None), P(("seg", "tp"), None), P(("seg", "tp"), None))
    return jax.shard_map(local, mesh=mesh, in_specs=in_specs, out_specs=out_specs, check_vma=False)
```

profile of v0, /device:TPU:1, one launch (start us, length us, event | category | flops | bytes accessed | tf_op | source)
XLA Modules:
  0.0 302.9 jit_solution(4560947407831496321)
XLA Ops:
  0.7 1.3 dynamic_slice.10
  2.1 1.3 broadcast_compare_fusion
  4.2 53.7 %all_gather.6 = bf16[2048,128]{1,0:T(8,128)(2,1)S(1)} all-gather(bf16[32,128]{1,0:T(8,128)(2,1)S(1)} %slice.58), channel_id=1, replica_groups=mesh['seg'=64,'tp'=8] {'seg'}, dimensions={0}, use_global_device_ids=true | all-gather | bytes 532480 | tf_op jit(solution)/shard_map/all_gather | solution.py:16
  59.5 50.2 %all_gather.7 = bf16[2048,128]{1,0:T(8,128)(2,1)S(1)} all-gather(bf16[32,128]{1,0:T(8,128)(2,1)S(1)} %slice.59), channel_id=1, replica_groups=mesh['seg'=64,'tp'=8] {'seg'}, dimensions={0}, use_global_device_ids=true | all-gather | bytes 532480 | tf_op jit(solution)/shard_map/all_gather | solution.py:17
  113.3 68.9 %while.17 = (s32[]{:T(128)}, f32[2304,128]{1,0:T(8,128)S(1)}, f32[2304,128]{1,0:T(8,128)}, bf16[4,512,128]{2,1,0:T(8,128)(2,1)}, bf16[4,512,128]{2,1,0:T(8,128)(...) while((s32[]{:T(128)}, f32[2304,128]{1,0:T(8,128)S(1)}, ...), condition=%wide.region_4.5_spmd.clone, body=%wide.region_0.4_spmd.clone.sunk | while | flops 1531607552 | bytes 88564424 | solution.py:68
  113.3 2.0 fusion.56
  115.3 2.1 copy-done.1
  118.2 4.7 %convolution_add_fusion.2 = f32[2304,128]{1,0:T(8,128)} fusion(f32[2304,128]{1,0:T(8,128)} %get-tuple-element.207, pred[]{:T(512)S(6)} %compare.13, bf16[4,512,128]{2,1,0:T(8,128)(2,1)} %get-tuple-element.223, s32[]{:T(128)} %get-tuple-element.205, f32[512,2304]{1,0:T(8,128)} %copy-done.1, f32[512]{0:T(512)S(1)} %fusion.57, ...), kind=kOutput, calls=%fused_computation.7.clone.1 | convolution fusion | flops 306118656 | bytes 7213569 | tf_op jit(solution)/shard_map/while/body/eval_jaxpr/dot_general | solution.py:55
  122.9 2.2 multiply_reduce_fusion.2
  125.1 1.5 multiply_convert_fusion.2
  126.6 2.1 fusion.58
  128.8 1.5 fusion.59
  130.2 2.0 fusion.56
  132.2 2.1 copy-done.1
  135.1 5.1 %convolution_add_fusion.2 = f32[2304,128]{1,0:T(8,128)} fusion(f32[2304,128]{1,0:T(8,128)} %get-tuple-element.207, pred[]{:T(512)S(6)} %compare.13, bf16[4,512,128]{2,1,0:T(8,128)(2,1)} %get-tuple-element.223, s32[]{:T(128)} %get-tuple-element.205, f32[512,2304]{1,0:T(8,128)} %copy-done.1, f32[512]{0:T(512)S(1)} %fusion.57, ...), kind=kOutput, calls=%fused_computation.7.clone.1 | convolution fusion | flops 306118656 | bytes 7213569 | tf_op jit(solution)/shard_map/while/body/eval_jaxpr/dot_general | solution.py:55
  140.2 2.2 multiply_reduce_fusion.2
  142.4 1.5 multiply_convert_fusion.2
  144.0 2.1 fusion.58
  146.1 1.4 fusion.59
  147.5 2.0 fusion.56
  149.5 2.1 copy-done.1
  152.4 5.1 %convolution_add_fusion.2 = f32[2304,128]{1,0:T(8,128)} fusion(f32[2304,128]{1,0:T(8,128)} %get-tuple-element.207, pred[]{:T(512)S(6)} %compare.13, bf16[4,512,128]{2,1,0:T(8,128)(2,1)} %get-tuple-element.223, s32[]{:T(128)} %get-tuple-element.205, f32[512,2304]{1,0:T(8,128)} %copy-done.1, f32[512]{0:T(512)S(1)} %fusion.57, ...), kind=kOutput, calls=%fused_computation.7.clone.1 | convolution fusion | flops 306118656 | bytes 7213569 | tf_op jit(solution)/shard_map/while/body/eval_jaxpr/dot_general | solution.py:55
  157.6 2.2 multiply_reduce_fusion.2
  159.8 1.5 multiply_convert_fusion.2
  161.3 2.1 fusion.58
  163.4 1.4 fusion.59
  164.9 2.0 fusion.56
  166.9 2.1 copy-done.1
  169.8 5.1 %convolution_add_fusion.2 = f32[2304,128]{1,0:T(8,128)} fusion(f32[2304,128]{1,0:T(8,128)} %get-tuple-element.207, pred[]{:T(512)S(6)} %compare.13, bf16[4,512,128]{2,1,0:T(8,128)(2,1)} %get-tuple-element.223, s32[]{:T(128)} %get-tuple-element.205, f32[512,2304]{1,0:T(8,128)} %copy-done.1, f32[512]{0:T(512)S(1)} %fusion.57, ...), kind=kOutput, calls=%fused_computation.7.clone.1 | convolution fusion | flops 306118656 | bytes 7213569 | tf_op jit(solution)/shard_map/while/body/eval_jaxpr/dot_general | solution.py:55
  174.9 2.2 multiply_reduce_fusion.2
  177.1 1.5 multiply_convert_fusion.2
  178.6 2.1 fusion.58
  180.8 1.4 fusion.59
  182.2 1.4 copy.43
  184.6 7.7 %all-to-all-start = ((bf16[8,32,1024]{2,1,0:T(8,128)(2,1)}), bf16[8,32,1024]{2,1,0:T(8,128)(2,1)S(1)}, u32[]{:S(2)}, u32[]{:S(2)}) async-start(bf16[8,32,1024]{2,1,0:T(8,128)(2,1)} %all_to_all.48), calls=%async_computation | async-start | bytes 1048576 | tf_op jit(solution)/shard_map/all_to_all | solution.py:101
  192.3 2.3 slice.71
  194.6 15.7 %all-to-all-done = bf16[8,32,1024]{2,1,0:T(8,128)(2,1)S(1)} async-done(((bf16[8,32,1024]{2,1,0:T(8,128)(2,1)}), bf16[8,32,1024]{2,1,0:T(8,128)(2,1)S(1)}, u32[]{:S(2)}, u32[]{:S(2)}) %all-to-all-start) | async-done | bytes 524320 | tf_op jit(solution)/shard_map/all_to_all | solution.py:101
  210.2 7.5 %all-to-all-start.3 = ((f32[64,32,128]{2,1,0:T(8,128)}), f32[64,32,128]{2,1,0:T(8,128)S(1)}, u32[]{:S(2)}, u32[]{:S(2)}) async-start(f32[64,32,128]{2,1,0:T(8,128)} %bitcast.110), calls=%async_computation.3 | async-start | bytes 2097152 | tf_op jit(solution)/shard_map/all_to_all | solution.py:88
  218.8 26.9 %all-to-all-done.3 = f32[64,32,128]{2,1,0:T(8,128)S(1)} async-done(((f32[64,32,128]{2,1,0:T(8,128)}), f32[64,32,128]{2,1,0:T(8,128)S(1)}, u32[]{:S(2)}, u32[]{:S(2)}) %all-to-all-start.3) | async-done | bytes 1048608 | tf_op jit(solution)/shard_map/all_to_all | solution.py:88
  246.8 6.5 %all-to-all-start.1 = ((f32[64,32,128]{2,1,0:T(8,128)}), f32[64,32,128]{2,1,0:T(8,128)S(1)}, u32[]{:S(2)}, u32[]{:S(2)}) async-start(f32[64,32,128]{2,1,0:T(8,128)} %bitcast.109), calls=%async_computation.1 | async-start | bytes 2097152 | tf_op jit(solution)/shard_map/all_to_all | solution.py:81
  253.3 1.5 slice_bitcast_fusion
  256.3 1.3 reduce_sum.37
  257.6 1.3 fusion.23
  258.9 22.3 %all-to-all-done.1 = f32[64,32,128]{2,1,0:T(8,128)S(1)} async-done(((f32[64,32,128]{2,1,0:T(8,128)}), f32[64,32,128]{2,1,0:T(8,128)S(1)}, u32[]{:S(2)}, u32[]{:S(2)}) %all-to-all-start.1) | async-done | bytes 1048608 | tf_op jit(solution)/shard_map/all_to_all | solution.py:81
  281.3 3.4 %all-to-all-start.4 = ((bf16[8,32,128]{2,1,0:T(8,128)(2,1)}), bf16[8,32,128]{2,1,0:T(8,128)(2,1)S(1)}, u32[]{:S(2)}, u32[]{:S(2)}) async-start(bf16[8,32,128]{2,1,0:T(8,128)(2,1)} %bitcast.18), calls=%async_computation.4 | async-start | bytes 131072 | tf_op jit(solution)/shard_map/all_to_all | solution.py:103
  285.3 6.4 %all-to-all-done.4 = bf16[8,32,128]{2,1,0:T(8,128)(2,1)S(1)} async-done(((bf16[8,32,128]{2,1,0:T(8,128)(2,1)}), bf16[8,32,128]{2,1,0:T(8,128)(2,1)S(1)}, u32[]{:S(2)}, u32[]{:S(2)}) %all-to-all-start.4) | async-done | bytes 65568 | tf_op jit(solution)/shard_map/all_to_all | solution.py:103
  291.8 3.4 %all-to-all-start.2 = ((bf16[8,32,128]{2,1,0:T(8,128)(2,1)}), bf16[8,32,128]{2,1,0:T(8,128)(2,1)S(1)}, u32[]{:S(2)}, u32[]{:S(2)}) async-start(bf16[8,32,128]{2,1,0:T(8,128)(2,1)} %bitcast.12), calls=%async_computation.2 | async-start | bytes 131072 | tf_op jit(solution)/shard_map/all_to_all | solution.py:102
  295.8 6.5 %all-to-all-done.2 = bf16[8,32,128]{2,1,0:T(8,128)(2,1)S(1)} async-done(((bf16[8,32,128]{2,1,0:T(8,128)(2,1)}), bf16[8,32,128]{2,1,0:T(8,128)(2,1)S(1)}, u32[]{:S(2)}, u32[]{:S(2)}) %all-to-all-start.2) | async-done | bytes 65568 | tf_op jit(solution)/shard_map/all_to_all | solution.py:102
  (54 shorter events, 15.6 us)
Async XLA Ops:
  0.6 110.0 %copy-start = (bf16[256,1024]{1,0:T(8,128)(2,1)S(1)}, bf16[256,1024]{1,0:T(8,128)(2,1)}, u32[]{:S(2)}) copy-start(bf16[256,1024]{1,0:T(8,128)(2,1)} %param.11) | copy-start | bytes 1572868
  0.6 109.1 %copy-start.6 = (bf16[256,128]{1,0:T(8,128)(2,1)S(1)}, bf16[256,128]{1,0:T(8,128)(2,1)}, u32[]{:S(2)}) copy-start(bf16[256,128]{1,0:T(8,128)(2,1)} %param.13) | copy-start | bytes 196612
  0.7 110.9 %copy-start.5 = (bf16[256,1024]{1,0:T(8,128)(2,1)S(1)}, bf16[256,1024]{1,0:T(8,128)(2,1)}, u32[]{:S(2)}) copy-start(bf16[256,1024]{1,0:T(8,128)(2,1)} %param.14) | copy-start | bytes 1572868
  115.3 2.1 copy-start.1
  118.2 4.7 %copy-start.2 = (f32[512,2304]{1,0:T(8,128)S(1)}, f32[512,2304]{1,0:T(8,128)}, u32[]{:S(2)}) copy-start(f32[512,2304]{1,0:T(8,128)} %copy-done.1) | copy-start | bytes 14155780 | tf_op jit(solution)/shard_map/while
  118.2 4.7 %copy-start.4 = (bf16[2304,128]{1,0:T(8,128)(2,1)S(1)}, bf16[2304,128]{1,0:T(8,128)(2,1)}, u32[]{:S(2)}) copy-start(bf16[2304,128]{1,0:T(8,128)(2,1)} %get-tuple-element.224) | copy-start | bytes 1769476 | tf_op jit(solution)/shard_map/while
  132.2 2.1 copy-start.1
  135.1 5.1 %copy-start.2 = (f32[512,2304]{1,0:T(8,128)S(1)}, f32[512,2304]{1,0:T(8,128)}, u32[]{:S(2)}) copy-start(f32[512,2304]{1,0:T(8,128)} %copy-done.1) | copy-start | bytes 14155780 | tf_op jit(solution)/shard_map/while
  135.1 5.1 %copy-start.4 = (bf16[2304,128]{1,0:T(8,128)(2,1)S(1)}, bf16[2304,128]{1,0:T(8,128)(2,1)}, u32[]{:S(2)}) copy-start(bf16[2304,128]{1,0:T(8,128)(2,1)} %get-tuple-element.224) | copy-start | bytes 1769476 | tf_op jit(solution)/shard_map/while
  149.5 2.1 copy-start.1
  152.4 5.1 %copy-start.2 = (f32[512,2304]{1,0:T(8,128)S(1)}, f32[512,2304]{1,0:T(8,128)}, u32[]{:S(2)}) copy-start(f32[512,2304]{1,0:T(8,128)} %copy-done.1) | copy-start | bytes 14155780 | tf_op jit(solution)/shard_map/while
  152.4 5.1 %copy-start.4 = (bf16[2304,128]{1,0:T(8,128)(2,1)S(1)}, bf16[2304,128]{1,0:T(8,128)(2,1)}, u32[]{:S(2)}) copy-start(bf16[2304,128]{1,0:T(8,128)(2,1)} %get-tuple-element.224) | copy-start | bytes 1769476 | tf_op jit(solution)/shard_map/while
  166.8 2.1 copy-start.1
  169.8 5.1 %copy-start.2 = (f32[512,2304]{1,0:T(8,128)S(1)}, f32[512,2304]{1,0:T(8,128)}, u32[]{:S(2)}) copy-start(f32[512,2304]{1,0:T(8,128)} %copy-done.1) | copy-start | bytes 14155780 | tf_op jit(solution)/shard_map/while
  169.8 5.1 %copy-start.4 = (bf16[2304,128]{1,0:T(8,128)(2,1)S(1)}, bf16[2304,128]{1,0:T(8,128)(2,1)}, u32[]{:S(2)}) copy-start(bf16[2304,128]{1,0:T(8,128)(2,1)} %get-tuple-element.224) | copy-start | bytes 1769476 | tf_op jit(solution)/shard_map/while
  184.6 25.6 %all-to-all-start = ((bf16[8,32,1024]{2,1,0:T(8,128)(2,1)}), bf16[8,32,1024]{2,1,0:T(8,128)(2,1)S(1)}, u32[]{:S(2)}, u32[]{:S(2)}) async-start(bf16[8,32,1024]{2,1,0:T(8,128)(2,1)} %all_to_all.48), calls=%async_computation | async-start | bytes 1048576 | tf_op jit(solution)/shard_map/all_to_all | solution.py:101
  210.2 35.5 %all-to-all-start.3 = ((f32[64,32,128]{2,1,0:T(8,128)}), f32[64,32,128]{2,1,0:T(8,128)S(1)}, u32[]{:S(2)}, u32[]{:S(2)}) async-start(f32[64,32,128]{2,1,0:T(8,128)} %bitcast.110), calls=%async_computation.3 | async-start | bytes 2097152 | tf_op jit(solution)/shard_map/all_to_all | solution.py:88
  245.8 1.0 copy-start.3
  246.8 34.5 %all-to-all-start.1 = ((f32[64,32,128]{2,1,0:T(8,128)}), f32[64,32,128]{2,1,0:T(8,128)S(1)}, u32[]{:S(2)}, u32[]{:S(2)}) async-start(f32[64,32,128]{2,1,0:T(8,128)} %bitcast.109), calls=%async_computation.1 | async-start | bytes 2097152 | tf_op jit(solution)/shard_map/all_to_all | solution.py:81
  281.3 10.5 %all-to-all-start.4 = ((bf16[8,32,128]{2,1,0:T(8,128)(2,1)}), bf16[8,32,128]{2,1,0:T(8,128)(2,1)S(1)}, u32[]{:S(2)}, u32[]{:S(2)}) async-start(bf16[8,32,128]{2,1,0:T(8,128)(2,1)} %bitcast.18), calls=%async_computation.4 | async-start | bytes 131072 | tf_op jit(solution)/shard_map/all_to_all | solution.py:103
  291.8 10.5 %all-to-all-start.2 = ((bf16[8,32,128]{2,1,0:T(8,128)(2,1)}), bf16[8,32,128]{2,1,0:T(8,128)(2,1)S(1)}, u32[]{:S(2)}, u32[]{:S(2)}) async-start(bf16[8,32,128]{2,1,0:T(8,128)(2,1)} %bitcast.12), calls=%async_computation.2 | async-start | bytes 131072 | tf_op jit(solution)/shard_map/all_to_all | solution.py:102
where the time goes:
time: 306 us; the launch traced here: 303 us
  blocking collectives  104 us (34%)
  waiting for transfers between devices  77.9 us (25%)
  matrix products  51.1 us (17%)
  starting transfers between devices  28.4 us (9%)
  local copies, waits for them, and re-layouts  24.4 us (8%)
  other arithmetic  16.2 us (5%)
    all_gather x1, blocking collectives, local(): lax.all_gather(key_rows[seg_len - SUMM:], 'seg', axis=0, tiled=True)  53.7 us
    all_gather x1, blocking collectives, local(): lax.all_gather(value_rows[seg_len - SUMM:], 'seg', axis=0, tiled=True)  50.2 us
    all_to_all x1, waiting for transfers between devices, local(): lax.all_to_all(prior_dv.reshape(slots, SUMM, kv_count * HEAD_DIM), 'seg',...  26.9 us
    all_to_all x1, waiting for transfers between devices, local(): lax.all_to_all(prior_dk.reshape(slots, SUMM, kv_count * HEAD_DIM), 'seg',...  22.3 us
    dot_general x4, matrix products, head_step(): lax.dot_general(probs_low, g_rows, contract_first, preferred_element_type...  20.1 us
    all_to_all x1, waiting for transfers between devices, local(): lax.all_to_all(dq_all, 'tp', split_axis=0, concat_axis=1, tiled=True)  15.7 us
    dot_general x4, matrix products, head_step(): lax.dot_general(g_rows, head_v, contract_last, preferred_element_type=jnp...  8.84 us
    while x24, local copies, waits for them, and re-layouts  8.56 us
  transfers between devices with their start and end apart: 5, of which 5 were waited for; matrix products, arithmetic and copies ran while one was open for 3% of the time, Pallas kernels for 0%

commit v1 on v0

v1 whole, which is shorter than its diff:
```python
import functools

import jax
import jax.numpy as jnp
from jax import lax
from jax.experimental import pallas as pl
from jax.experimental.pallas import tpu as pltpu
from jax.sharding import PartitionSpec as P

HEAD_DIM = 128
SUMM = 32
SEG = 256
NY, NX, NZ = 8, 4, 8
GROUP = 8
CHUNKS = 9
SCALE = HEAD_DIM**-0.5
SCALE_LOG2 = SCALE * 1.4426950408889634
HIDDEN = -1e30
BF = jnp.bfloat16
F32 = jnp.float32
MESH = pl.DeviceIdType.MESH


def dot(a, b):
    return jnp.dot(a, b, preferred_element_type=F32)


def dot_t(a, b):
    return lax.dot_general(a, b, (((1,), (1,)), ((), ())), preferred_element_type=F32)


def kernel(
    order_ref, q_ref, k_ref, v_ref, g_ref, oq_ref, ok_ref, ov_ref,
    bias, buf, s_ref, dp_ref, e_ref, ds_ref, qp_ref, gp_ref, kt_ref, dq_ref,
    sib_out, sib_in, x_out, x_in, x_own, y_out, y_in, local, summ, final,
    gy_s, gy_r, gx_s, gx_r, gs_s, gs_r, rs_s, rs_r, rx_s, rx_r, ry_s, ry_r, q_s, q_r, k_s, k_r, v_s, v_r,
):
    seg = lax.axis_index("seg")
    z = lax.axis_index("tp")
    core = lax.rem(seg, 2)
    x = lax.rem(seg // 2, NX)
    y = seg // (2 * NX)
    mine = x * 2 + core

    def seg_dev(yy, xx, cc):
        return {"seg": (yy * NX + xx) * 2 + cc}

    def y_dev(r):
        return seg_dev(lax.rem(y + r, NY), x, core)

    def x_dev(r):
        return seg_dev(y, lax.rem(x + r, NX), core)

    def z_dev(r):
        return {"tp": lax.rem(z + r, NZ)}

    sibling = seg_dev(y, x, 1 - core)

    def remote(src, dst, send, recv, dev):
        return pltpu.make_async_remote_copy(
            src_ref=src, dst_ref=dst, send_sem=send, recv_sem=recv, device_id=dev, device_id_type=MESH
        )

    barrier = pltpu.get_barrier_semaphore()
    peers = [y_dev(r) for r in range(1, NY)] + [x_dev(r) for r in range(1, NX)]
    peers += [sibling] + [z_dev(r) for r in range(1, NZ)]
    for dev in peers:
        pl.semaphore_signal(barrier, inc=1, device_id=dev, device_id_type=MESH)
    pl.semaphore_wait(barrier, len(peers))

    buf[mine, y, 0] = k_ref[SEG - SUMM :, :]
    buf[mine, y, 1] = v_ref[SEG - SUMM :, :]
    gy = {}
    for r in (4, 3, 5, 2, 6, 1, 7):
        gy[r] = remote(buf.at[mine, y], buf.at[mine, y], gy_s.at[r], gy_r.at[r], y_dev(r))
        gy[r].start()
    own = order_ref[seg]
    for xc in range(2 * NX):
        for yy in range(NY):
            bias[xc * NY + yy] = jnp.where(order_ref[yy * 2 * NX + xc] < own, 0.0, HIDDEN)
    kt_ref[:, :SEG] = k_ref[...].T
    for r in range(1, NY):
        gy[r].wait_recv()
    gx = {}
    for r in (2, 1, 3):
        gx[r] = remote(buf.at[mine], buf.at[mine], gx_s.at[r], gx_r.at[r], x_dev(r))
        gx[r].start()
    gs = {0: remote(buf.at[mine], buf.at[mine], gs_s.at[0], gs_r.at[0], sibling)}
    gs[0].start()
    for r in (1, 3, 2):
        gx[r].wait_recv()
        block = lax.rem(x + NX - r, NX) * 2 + core
        gs[r] = remote(buf.at[block], buf.at[block], gs_s.at[r], gs_r.at[r], sibling)
        gs[r].start()
    for r in range(NX):
        gs[r].wait_recv()
    for r in range(1, NY):
        gy[r].wait_send()
    for r in range(1, NX):
        gx[r].wait_send()
    for r in range(NX):
        gs[r].wait_send()

    def keys(c):
        return k_ref[...] if c == 0 else buf[c - 1, :, 0].reshape(SEG, HEAD_DIM)

    def values(c):
        return v_ref[...] if c == 0 else buf[c - 1, :, 1].reshape(SEG, HEAD_DIM)

    for c in range(1, CHUNKS):
        kt_ref[:, c * SEG : (c + 1) * SEG] = keys(c).T

    def fold(a, op):
        return op(a.reshape(SEG // 8, 8, SEG), 0)

    def dq_copy(h, r):
        to = lax.rem(z + r, NZ)
        return remote(
            dq_ref.at[h, pl.ds(to * SUMM, SUMM), :],
            oq_ref.at[:, pl.ds(pl.multiple_of((z * GROUP + h) * HEAD_DIM, HEAD_DIM), HEAD_DIM)],
            q_s.at[r], q_r.at[r], z_dev(r),
        )

    def head(h, carry):
        cols = pl.ds(pl.multiple_of(h * HEAD_DIM, HEAD_DIM), HEAD_DIM)
        wide = pl.ds(pl.multiple_of(h * SEG, SEG), SEG)
        qh = q_ref[:, cols]
        gh = g_ref[:, cols]
        top = jnp.full((8, SEG), HIDDEN, F32)
        for c in range(CHUNKS):
            rows = slice(c * SEG, (c + 1) * SEG)
            s = dot_t(keys(c), qh)
            if c == 0:
                key_pos = lax.broadcasted_iota(jnp.int32, (SEG, SEG), 0)
                query_pos = lax.broadcasted_iota(jnp.int32, (SEG, SEG), 1)
                s = jnp.where(key_pos <= query_pos, s, HIDDEN)
            else:
                s = jnp.concatenate(
                    [s[SUMM * t : SUMM * (t + 1)] + bias[(c - 1) * NY + t] for t in range(NY)], 0
                )
            s_ref[rows, :] = s
            top = jnp.maximum(top, fold(s, jnp.max))
        top = jnp.max(top, 0, keepdims=True) * SCALE_LOG2
        total = jnp.zeros((8, SEG), F32)
        delta = jnp.zeros((8, SEG), F32)
        for c in range(CHUNKS):
            rows = slice(c * SEG, (c + 1) * SEG)
            e = jnp.exp2(s_ref[rows, :] * SCALE_LOG2 - top)
            dp = dot_t(values(c), gh)
            total = total + fold(e, jnp.sum)
            delta = delta + fold(e * dp, jnp.sum)
            e_ref[rows, wide] = e.astype(BF)
            dp_ref[rows, :] = dp
        inv = 1.0 / jnp.sum(total, 0, keepdims=True)
        delta = jnp.sum(delta, 0, keepdims=True) * inv
        acc = jnp.zeros((HEAD_DIM, SEG), F32)
        for c in range(CHUNKS):
            rows = slice(c * SEG, (c + 1) * SEG)
            ds = (e_ref[rows, wide].astype(F32) * (dp_ref[rows, :] - delta)).astype(BF)
            ds_ref[rows, wide] = ds
            acc = acc + dot(kt_ref[:, rows], ds)
        dq_ref[h] = (acc * (inv * SCALE)).T.astype(BF)
        for r in (4, 3, 5, 2, 6, 1, 7):
            dq_copy(h, r).start()
        inv_rows = jnp.broadcast_to(inv, (HEAD_DIM, SEG)).T
        qp_ref[wide, :] = (qh.astype(F32) * (inv_rows * SCALE)).astype(BF)
        gp_ref[wide, :] = (gh.astype(F32) * inv_rows).astype(BF)
        return carry

    lax.fori_loop(0, GROUP, head, 0)

    def terms(c):
        rows = pl.ds(pl.multiple_of(c * SEG, SEG), SEG)
        return dot(ds_ref[rows, :], qp_ref[...]), dot(e_ref[rows, :], gp_ref[...])

    def split(a):
        return a.reshape(NY, SUMM, HEAD_DIM)

    rs, rx, ry = {}, {}, {}
    for r in (2, 1, 3, 0):
        xx = lax.rem(x + r, NX)
        dk, dv = terms(1 + xx * 2 + 1 - core)
        sib_out[r, :, 0] = split(dk).astype(BF)
        sib_out[r, :, 1] = split(dv).astype(BF)
        rs[r] = remote(sib_out.at[r], sib_in.at[r], rs_s.at[r], rs_r.at[r], sibling)
        rs[r].start()
        dk, dv = terms(1 + xx * 2 + core)
        rs[r].wait_recv()
        dk = split(dk) + sib_in[r, :, 0].astype(F32)
        dv = split(dv) + sib_in[r, :, 1].astype(F32)
        if r:
            x_out[r, :, 0] = dk.astype(BF)
            x_out[r, :, 1] = dv.astype(BF)
            rx[r] = remote(x_out.at[r], x_in.at[r], rx_s.at[r], rx_r.at[r], x_dev(r))
            rx[r].start()
        else:
            x_own[:, 0] = dk
            x_own[:, 1] = dv
    dk, dv = terms(0)
    local[0] = dk.astype(BF)
    local[1] = dv.astype(BF)
    summ[0] = dk[SEG - SUMM :]
    summ[1] = dv[SEG - SUMM :]

    my_cols = pl.ds(pl.multiple_of(z * HEAD_DIM, HEAD_DIM), HEAD_DIM)

    def kv_copies(r, src_k, src_v):
        return (
            remote(src_k, ok_ref.at[:, my_cols], k_s.at[r], k_r.at[r], z_dev(r)),
            remote(src_v, ov_ref.at[:, my_cols], v_s.at[r], v_r.at[r], z_dev(r)),
        )

    def early(r):
        rows = pl.ds(lax.rem(z + r, NZ) * SUMM, SUMM)
        return kv_copies(r, local.at[0, rows, :], local.at[1, rows, :])

    for r in range(1, NZ):

        @pl.when(lax.rem(z + r, NZ) != NZ - 1)
        def _(r=r):
            for copy in early(r):
                copy.start()

    for r in (1, 3, 2):
        rx[r].wait_recv()
    acc = x_own[...]
    for r in range(1, NX):
        acc = acc + x_in[r].astype(F32)
    x_own[...] = acc
    y_out[...] = acc.astype(BF)
    for r in (4, 3, 5, 2, 6, 1, 7):
        ry[r] = remote(y_out.at[lax.rem(y + r, NY)], y_in.at[r], ry_s.at[r], ry_r.at[r], y_dev(r))
        ry[r].start()
    acc = x_own[y] + summ[...]
    for r in range(1, NY):
        ry[r].wait_recv()
        acc = acc + y_in[r].astype(F32)
    final[...] = acc.astype(BF)
    for r in range(1, NZ):

        @pl.when(lax.rem(z + r, NZ) == NZ - 1)
        def _(r=r):
            for copy in kv_copies(r, final.at[0], final.at[1]):
                copy.start()

    my_rows = pl.ds(z * SUMM, SUMM)
    oq_cols = pl.ds(pl.multiple_of(z * GROUP * HEAD_DIM, GROUP * HEAD_DIM), GROUP * HEAD_DIM)
    oq_ref[:, oq_cols] = jnp.concatenate([dq_ref[h, my_rows, :] for h in range(GROUP)], 1)

    @pl.when(z != NZ - 1)
    def _():
        ok_ref[:, my_cols] = local[0, my_rows, :]
        ov_ref[:, my_cols] = local[1, my_rows, :]

    @pl.when(z == NZ - 1)
    def _():
        ok_ref[:, my_cols] = final[0]
        ov_ref[:, my_cols] = final[1]

    for r in range(1, NZ):
        for copy in early(r):
            copy.wait()
        whole = remote(oq_ref.at[:, oq_cols], oq_ref.at[:, oq_cols], q_s.at[r], q_r.at[r], z_dev(r))
        whole.wait()
    for r in range(NX):
        rs[r].wait_send()
    for r in range(1, NX):
        rx[r].wait_send()
    for r in range(1, NY):
        ry[r].wait_send()


def local(queries, key_rows, value_rows, grad_out, seg_order):
    vmem = pl.BlockSpec(memory_space=pltpu.VMEM)
    smem = pl.BlockSpec(memory_space=pltpu.SMEM)
    width = CHUNKS * SEG
    block = (NY, 2, SUMM, HEAD_DIM)
    sems = [NY, NY, NX, NX, NX, NX, NX, NX, NX, NX, NY, NY, NZ, NZ, NZ, NZ, NZ, NZ]
    return pl.pallas_call(
        kernel,
        out_shape=[
            jax.ShapeDtypeStruct((SUMM, NZ * GROUP * HEAD_DIM), BF),
            jax.ShapeDtypeStruct((SUMM, NZ * HEAD_DIM), BF),
            jax.ShapeDtypeStruct((SUMM, NZ * HEAD_DIM), BF),
        ],
        in_specs=[smem, vmem, vmem, vmem, vmem],
        out_specs=[vmem, vmem, vmem],
        scratch_shapes=[
            pltpu.SMEM((2 * NX * NY,), F32),
            pltpu.VMEM((2 * NX,) + block, BF),
            pltpu.VMEM((width, SEG), F32),
            pltpu.VMEM((width, SEG), F32),
            pltpu.VMEM((width, GROUP * SEG), BF),
            pltpu.VMEM((width, GROUP * SEG), BF),
            pltpu.VMEM((GROUP * SEG, HEAD_DIM), BF),
            pltpu.VMEM((GROUP * SEG, HEAD_DIM), BF),
            pltpu.VMEM((HEAD_DIM, width), BF),
            pltpu.VMEM((GROUP, SEG, HEAD_DIM), BF),
            pltpu.VMEM((NX,) + block, BF),
            pltpu.VMEM((NX,) + block, BF),
            pltpu.VMEM((NX,) + block, BF),
            pltpu.VMEM((NX,) + block, BF),
            pltpu.VMEM(block, F32),
            pltpu.VMEM(block, BF),
            pltpu.VMEM(block, BF),
            pltpu.VMEM((2, SEG, HEAD_DIM), BF),
            pltpu.VMEM((2, SUMM, HEAD_DIM), F32),
            pltpu.VMEM((2, SUMM, HEAD_DIM), BF),
        ]
        + [pltpu.SemaphoreType.DMA((n,)) for n in sems],
        compiler_params=pltpu.CompilerParams(
            collective_id=0, has_side_effects=True, vmem_limit_bytes=56 * 2**20
        ),
        name="attention_backward",
    )(seg_order, queries, key_rows, value_rows, grad_out)


def solution(mesh):
    in_specs = (P("seg", "tp"), P("seg", "tp"), P("seg", "tp"), P("seg", "tp"), P())
    out_specs = (P(("seg", "tp"), None), P(("seg", "tp"), None), P(("seg", "tp"), None))
    return jax.shard_map(local, mesh=mesh, in_specs=in_specs, out_specs=out_specs, check_vma=False)
```

time: 306 us -> 71.5 us (0.23)
  blocking collectives: 104 us -> 0 us
  waiting for transfers between devices: 77.9 us -> 0 us
  Pallas kernels: 0 us -> 67.2 us
  matrix products: 51.1 us -> 0 us
  starting transfers between devices: 28.4 us -> 0 us
  local copies, waits for them, and re-layouts: 24.4 us -> 3.4 us
  other arithmetic: 16.2 us -> 0 us
    all_gather x2 -> x0, blocking collectives: 104 us -> none  [the longest x1 53.7 us: local(): lax.all_gather(key_rows[seg_len - SUMM:], 'seg', axis=0, tiled=True)]
    all_to_all x5 -> x0, waiting for transfers between devices: 77.9 us -> none  [the longest x1 26.9 us: local(): lax.all_to_all(prior_dv.reshape(slots, SUMM, kv_count * HEAD_DIM), 'seg',...]
    pallas_call x0 -> x1, Pallas kernels: none -> 67.2 us  [local(): pl.pallas_call(kernel, out_shape=[jax.ShapeDtypeStruct((SUMM, NZ * GROUP...]
    dot_general x20 -> x0, matrix products: 51.1 us -> none  [the longest x4 20.1 us: head_step(): lax.dot_general(probs_low, g_rows, contract_first, preferred_element_type...]
    all_to_all x5 -> x0, starting transfers between devices: 28.4 us -> none  [the longest x1 7.67 us: local(): lax.all_to_all(dq_all, 'tp', split_axis=0, concat_axis=1, tiled=True)]
    while x24 -> x0, local copies, waits for them, and re-layouts: 8.56 us -> none
    convert_element_type x4 -> x0, other arithmetic: 6 us -> none  [head_step(): grad_scores = (probs * (grad_probs - delta_rows)).astype(jnp.bfloat16)]
    another operation x5 -> x0, local copies, waits for them, and re-layouts: 5.34 us -> none  [the longest x1 1.54 us: local(): dv_stack[:, :seg_len].transpose(1, 0, 2)]
  transfers between devices with their start and end apart: 5 -> 0, of which waited for: 5 -> 0; matrix products, arithmetic and copies ran while one was open for 3% -> 0% of each run, Pallas kernels for 0% -> 0%
where the time goes in v1:
time: 71.5 us; the launch traced here: 71.3 us
  Pallas kernels  67.2 us (94%)
  local copies, waits for them, and re-layouts  3.4 us (5%)
    pallas_call x1, Pallas kernels, local(): pl.pallas_call(kernel, out_shape=[jax.ShapeDtypeStruct((SUMM, NZ * GROUP...  67.2 us
    unnamed x7, local copies, waits for them, and re-layouts  3.4 us

profile of v1, /device:TPU:1, one launch (start us, length us, event | category | flops | bytes accessed | tf_op | source)
XLA Modules:
  0.0 71.3 jit_solution(17965710626994936931)
XLA Ops:
  0.6 67.2 %attention_backward.1 = (bf16[32,8192]{1,0:T(8,128)(2,1)}, bf16[32,1024]{1,0:T(8,128)(2,1)}, bf16[32,1024]{1,0:T(8,128)(2,1)}) custom-call(s32[64]{0:T(128)} %order_ref.1, bf16[256,1024]{1,0:T(8,128)(2,1)} %q_ref.1, bf16[256,128]{1,0:T(8,128)(2,1)} %k_ref.1, bf16[256,128]{1,0:T(8,128)(2,1)} %v_ref.1, bf16[256,1024]{1,0:T(8,128)(2,1)} %g_ref.1), custom_call_target="tpu_custom_call" | custom-call | tf_op jit(solution)/shard_map/attention_backward/pallas_call | solution.py:279
  67.9 0.0 copy-start.1
  67.9 1.9 %copy.11 = bf16[32,8192]{1,0:T(8,128)(2,1)} copy(bf16[32,8192]{1,0:T(8,128)(2,1)} %get-tuple-element.6) | data formatting | bytes 1048576
  69.8 0.0 copy-done.1
  69.8 0.0 copy-start
  69.8 0.6 copy.12
  70.4 0.2 copy-done
  70.7 0.6 copy.13
Async XLA Ops:
  67.9 1.9 %copy-start.1 = (bf16[32,1024]{1,0:T(8,128)(2,1)S(1)}, bf16[32,1024]{1,0:T(8,128)(2,1)}, u32[]{:S(2)}) copy-start(bf16[32,1024]{1,0:T(8,128)(2,1)} %get-tuple-element.7) | copy-start | bytes 196612
  69.8 0.9 %copy-start = (bf16[32,1024]{1,0:T(8,128)(2,1)S(1)}, bf16[32,1024]{1,0:T(8,128)(2,1)}, u32[]{:S(2)}) copy-start(bf16[32,1024]{1,0:T(8,128)(2,1)} %get-tuple-element.8) | copy-start | bytes 196612

commit v2 on v0

v2 whole, which is shorter than its diff:
```python
import jax
import jax.numpy as jnp
from jax import lax
from jax.experimental import pallas as pl
from jax.experimental.pallas import tpu as pltpu
from jax.sharding import PartitionSpec as P

HEAD_DIM = 128
SUMM = 32
SEG = 256
NY, NX, NZ = 8, 4, 8
GROUP = 8
CHUNKS = 9
SCALE = HEAD_DIM**-0.5
SCALE_LOG2 = SCALE * 1.4426950408889634
HIDDEN = -1e30
BF = jnp.bfloat16
F32 = jnp.float32
MESH = pl.DeviceIdType.MESH
KEYS, VALUES = 0, 1
FAR_FIRST = (4, 3, 5, 2, 6, 1, 7)


def dot(a, b):
    return jnp.dot(a, b, preferred_element_type=F32)


def dot_t(a, b):
    return lax.dot_general(a, b, (((1,), (1,)), ((), ())), preferred_element_type=F32)


def split(a):
    return a.reshape(NY, SUMM, HEAD_DIM)


def fold(a, op):
    return op(a.reshape(SEG // 8, 8, SEG), 0)


def rows_of(slot):
    return slice(slot * SEG, (slot + 1) * SEG)


def aligned(index, size):
    return pl.ds(pl.multiple_of(index * size, size), size)


def kernel(
    order_ref, q_hbm, k_hbm, v_hbm, g_hbm, oq_ref, ok_ref, ov_ref,
    bias, q_ref, k_ref, v_ref, g_ref, buf, s_ref, dp_ref, e_ref, qp_ref, gp_ref, kt_ref, dq_ref,
    top_ref, inv_ref, delta_ref,
    sib_out, sib_in, parts, x_out, x_in, x_own, y_out, y_in, local, summ, final,
    in_sem, own_sem, gy_s, gy_r, gx_s, gx_r, gs_s, gs_r,
    rs_s, rs_r, rx_s, rx_r, ry_s, ry_r, q_s, q_r, z_s, z_r,
):
    seg = lax.axis_index("seg")
    z = lax.axis_index("tp")
    core = lax.rem(seg, 2)
    x = lax.rem(seg // 2, NX)
    y = seg // (2 * NX)

    def seg_dev(yy, xx, cc):
        return {"seg": (yy * NX + xx) * 2 + cc}

    def y_dev(r):
        return seg_dev(lax.rem(y + r, NY), x, core)

    def x_dev(r):
        return seg_dev(y, lax.rem(x + r, NX), core)

    def z_dev(r):
        return {"tp": lax.rem(z + r, NZ)}

    sibling = seg_dev(y, x, 1 - core)

    def column(d, cc):
        return lax.rem(x + d, NX) * 2 + cc

    def remote(src, dst, send, recv, dev):
        return pltpu.make_async_remote_copy(
            src_ref=src, dst_ref=dst, send_sem=send, recv_sem=recv, device_id=dev, device_id_type=MESH
        )

    mine = column(0, core)
    fetch = [
        pltpu.make_async_copy(k_hbm.at[pl.ds(SEG - SUMM, SUMM), :], buf.at[KEYS, mine, y], in_sem.at[0]),
        pltpu.make_async_copy(v_hbm.at[pl.ds(SEG - SUMM, SUMM), :], buf.at[VALUES, mine, y], in_sem.at[1]),
        pltpu.make_async_copy(k_hbm, k_ref, in_sem.at[2]),
        pltpu.make_async_copy(q_hbm, q_ref, in_sem.at[3]),
        pltpu.make_async_copy(v_hbm, v_ref, in_sem.at[4]),
        pltpu.make_async_copy(g_hbm, g_ref, in_sem.at[5]),
    ]
    for copy in fetch:
        copy.start()
    barrier = pltpu.get_barrier_semaphore()
    peers = [y_dev(r) for r in range(1, NY)] + [x_dev(r) for r in range(1, NX)]
    peers += [sibling] + [z_dev(r) for r in range(1, NZ)]
    for dev in peers:
        pl.semaphore_signal(barrier, inc=1, device_id=dev, device_id_type=MESH)
    sends = []

    def go(copy):
        copy.start()
        sends.append(copy)
        return copy

    fetch[0].wait()
    fetch[1].wait()
    pl.semaphore_wait(barrier, len(peers))

    gy, gs = {}, {}
    for t in (KEYS, VALUES):
        for r in FAR_FIRST:
            gy[t, r] = go(
                remote(buf.at[t, mine, y], buf.at[t, mine, y], gy_s.at[t, r], gy_r.at[t, r], y_dev(r))
            )

    def spread_x(t, block):
        for r in (2, 1, 3):
            remote(block, block, gx_s.at[t, r], gx_r.at[t, r], x_dev(r)).start()

    def column_x(t, r):
        block = buf.at[t, mine]
        return remote(block, block, gx_s.at[t, r], gx_r.at[t, r], x_dev(r))

    def to_sibling(t, d):
        block = buf.at[t, column(d, core)]
        gs[t, d] = go(remote(block, block, gs_s.at[t, d], gs_r.at[t, d], sibling))

    def gather_y(t):
        spread_x(t, buf.at[t, mine, y])
        for r in (1, 7, 2, 6, 3, 5, 4):
            gy[t, r].wait_recv()
            spread_x(t, buf.at[t, mine, lax.rem(y + NY - r, NY)])
        to_sibling(t, 0)
        for r in range(1, NX):
            sends.append(column_x(t, r))

    def gather_x(t, d):
        column_x(t, NX - d).wait_recv()
        to_sibling(t, d)

    def block_of(slot):
        return column((slot - 1) // 2, core if slot % 2 else 1 - core)

    def fetched(t, slot):
        if slot == 0:
            return (k_ref if t == KEYS else v_ref)[...]
        return buf[t, block_of(slot)].reshape(SEG, HEAD_DIM)

    def scores(slot):
        kc = fetched(KEYS, slot)
        rows = rows_of(slot)
        kt_ref[:, rows] = kc.T
        for h in range(GROUP):
            s = dot_t(kc, q_ref[:, h * HEAD_DIM : (h + 1) * HEAD_DIM]) * SCALE_LOG2
            if slot:
                s = jnp.concatenate(
                    [s[SUMM * i : SUMM * (i + 1)] + bias[block_of(slot) * NY + i] for i in range(NY)], 0
                )
            else:
                key_pos = lax.broadcasted_iota(jnp.int32, (SEG, SEG), 0)
                query_pos = lax.broadcasted_iota(jnp.int32, (SEG, SEG), 1)
                s = jnp.where(key_pos <= query_pos, s, HIDDEN)
            s_ref[h, rows, :] = s
            top = fold(s, jnp.max)
            top_ref[h] = jnp.maximum(top_ref[h], top) if slot else top

    def mask_terms():
        own = order_ref[seg]
        for xc in range(2 * NX):
            for yy in range(NY):
                bias[xc * NY + yy] = jnp.where(order_ref[yy * 2 * NX + xc] < own, 0.0, HIDDEN)

    mask_terms()
    for copy in fetch[2:]:
        copy.wait()
    scores(0)
    gather_y(KEYS)
    scores(1)
    gs[KEYS, 0].wait_recv()
    scores(2)
    gather_y(VALUES)
    for d in (3, 1, 2):
        gather_x(KEYS, d)
    scores(7)
    scores(3)
    scores(5)
    for d in (3, 1, 2):
        gs[KEYS, d].wait_recv()
    scores(8)
    scores(4)
    scores(6)

    def weigh(h):
        cols = aligned(h, HEAD_DIM)
        wide = aligned(h, SEG)
        top = jnp.max(top_ref[h], 0, keepdims=True)
        total = jnp.zeros((8, SEG), F32)
        for slot in range(CHUNKS):
            rows = rows_of(slot)
            e = jnp.exp2(s_ref[h, rows, :] - top)
            total = total + fold(e, jnp.sum)
            e_ref[rows, wide] = e.astype(BF)
        inv = 1.0 / jnp.sum(total, 0, keepdims=True)
        inv_ref[h] = inv
        inv_rows = jnp.broadcast_to(inv, (HEAD_DIM, SEG)).T
        qp_ref[wide, :] = (q_ref[:, cols].astype(F32) * (inv_rows * SCALE)).astype(BF)
        gp_ref[wide, :] = (g_ref[:, cols].astype(F32) * inv_rows).astype(BF)

    def weigh_pair(i, carry):
        weigh(2 * i)
        weigh(2 * i + 1)
        return carry

    lax.fori_loop(0, GROUP // 2, weigh_pair, 0)

    def weigh_products(h):
        cols = aligned(h, HEAD_DIM)
        wide = aligned(h, SEG)
        gh = g_ref[:, cols]
        delta = jnp.zeros((8, SEG), F32)
        for slot in range(CHUNKS):
            rows = rows_of(slot)
            dp = dot_t(fetched(VALUES, slot), gh)
            delta = delta + fold(e_ref[rows, wide].astype(F32) * dp, jnp.sum)
            dp_ref[h, rows, :] = dp
        delta_ref[h] = jnp.sum(delta, 0, keepdims=True) * inv_ref[h]

    def products_pair(i, carry):
        weigh_products(2 * i)
        weigh_products(2 * i + 1)
        return carry

    my_cols = aligned(z, HEAD_DIM)
    my_rows = pl.ds(z * SUMM, SUMM)
    outs = (ok_ref, ov_ref)

    def terms(t, slot):
        return dot(e_ref[rows_of(slot), :], (qp_ref if t == KEYS else gp_ref)[...])

    rs, rx, ry = {}, {}, {}

    def z_copy(t, r, src):
        return remote(src, outs[t].at[:, my_cols], z_s.at[t, r], z_r.at[t, r], z_dev(r))

    def early(t, r):
        return z_copy(t, r, local.at[t, pl.ds(lax.rem(z + r, NZ) * SUMM, SUMM), :])

    def score_grads(slot):
        rows = rows_of(slot)
        for h in range(GROUP):
            wide = slice(h * SEG, (h + 1) * SEG)
            e_ref[rows, wide] = (
                e_ref[rows, wide].astype(F32) * (dp_ref[h, rows, :] - delta_ref[h])
            ).astype(BF)

    def reduce_x(t):
        for d in (2, 1, 3, 0):
            sib_out[t, d] = split(terms(t, 2 + 2 * d)).astype(BF)
        for d in (2, 1, 3, 0):
            rs[t, d] = go(remote(sib_out.at[t, d], sib_in.at[t, d], rs_s.at[t, d], rs_r.at[t, d], sibling))
        for d in (2, 1, 3, 0):
            parts[d] = split(terms(t, 1 + 2 * d))
        for d in (2, 1, 3, 0):
            rs[t, d].wait_recv()
            part = parts[d] + sib_in[t, d].astype(F32)
            if d:
                x_out[t, d] = part.astype(BF)
                rx[t, d] = go(remote(x_out.at[t, d], x_in.at[t, d], rx_s.at[t, d], rx_r.at[t, d], x_dev(d)))
            else:
                x_own[t] = part
        part = terms(t, 0)
        local[t] = part.astype(BF)
        summ[t] = part[SEG - SUMM :]
        for r in range(1, NZ):

            @pl.when(lax.rem(z + r, NZ) != NZ - 1)
            def _(r=r):
                early(t, r).start()

    def reduce_y(t):
        acc = x_own[t]
        for d in (1, 3, 2):
            rx[t, d].wait_recv()
            acc = acc + x_in[t, d].astype(F32)
        x_own[t] = acc
        y_out[t] = acc.astype(BF)
        for r in FAR_FIRST:
            ry[t, r] = go(
                remote(y_out.at[t, lax.rem(y + r, NY)], y_in.at[t, r], ry_s.at[t, r], ry_r.at[t, r], y_dev(r))
            )

    def reduce_end(t):
        acc = x_own[t, y] + summ[t]
        for r in range(1, NY):
            ry[t, r].wait_recv()
            acc = acc + y_in[t, r].astype(F32)
        final[t] = acc.astype(BF)
        for r in range(1, NZ):

            @pl.when(lax.rem(z + r, NZ) == NZ - 1)
            def _(r=r):
                z_copy(t, r, final.at[t]).start()

        @pl.when(z != NZ - 1)
        def _():
            pltpu.make_async_copy(local.at[t, my_rows, :], outs[t].at[:, my_cols], own_sem.at[t]).start()

        @pl.when(z == NZ - 1)
        def _():
            pltpu.make_async_copy(final.at[t], outs[t].at[:, my_cols], own_sem.at[t]).start()

    def dq_cols(h):
        return aligned(z * GROUP + h, HEAD_DIM)

    def query_grads(first):
        for h in (first, first + 1):
            acc = dot(kt_ref[...], e_ref[:, h * SEG : (h + 1) * SEG])
            dq_ref[h] = (acc * (inv_ref[h] * SCALE)).T.astype(BF)
        for h in (first, first + 1):
            for r in FAR_FIRST:
                to = pl.ds(lax.rem(z + r, NZ) * SUMM, SUMM)
                remote(dq_ref.at[h, to, :], oq_ref.at[:, dq_cols(h)], q_s.at[r], q_r.at[r], z_dev(r)).start()

    for d in (3, 1, 2):
        gather_x(VALUES, d)
    reduce_x(VALUES)
    for d in range(NX):
        gs[VALUES, d].wait_recv()
    lax.fori_loop(0, GROUP // 2, products_pair, 0)
    for slot in range(CHUNKS):
        score_grads(slot)
    query_grads(0)
    reduce_y(VALUES)
    reduce_x(KEYS)
    query_grads(2)
    query_grads(4)
    query_grads(6)
    own_dq = [
        pltpu.make_async_copy(dq_ref.at[h, my_rows, :], oq_ref.at[:, dq_cols(h)], in_sem.at[h])
        for h in range(GROUP)
    ]
    for copy in own_dq:
        copy.start()
    reduce_end(VALUES)
    reduce_y(KEYS)
    reduce_end(KEYS)

    for copy in own_dq:
        copy.wait()
    oq_cols = aligned(z, GROUP * HEAD_DIM)
    for r in range(1, NZ):
        remote(oq_ref.at[:, oq_cols], oq_ref.at[:, oq_cols], q_s.at[r], q_r.at[r], z_dev(r)).wait()
    for t in (VALUES, KEYS):
        for r in range(1, NZ):
            early(t, r).wait()
        pltpu.make_async_copy(final.at[t], outs[t].at[:, my_cols], own_sem.at[t]).wait()
    for copy in sends:
        copy.wait_send()


def place(a_ref, b_ref, c_ref, oa_ref, ob_ref, oc_ref, sem):
    copies = [
        pltpu.make_async_copy(src, dst, sem.at[i])
        for i, (src, dst) in enumerate(((a_ref, oa_ref), (b_ref, ob_ref), (c_ref, oc_ref)))
    ]
    for copy in copies:
        copy.start()
    for copy in copies:
        copy.wait()


def backward(queries, key_rows, value_rows, grad_out, seg_order):
    hbm = pl.BlockSpec(memory_space=pl.ANY)
    smem = pl.BlockSpec(memory_space=pltpu.SMEM)
    width = CHUNKS * SEG
    column = (NY, SUMM, HEAD_DIM)
    outs = [
        jax.ShapeDtypeStruct((SUMM, NZ * GROUP * HEAD_DIM), BF),
        jax.ShapeDtypeStruct((SUMM, NZ * HEAD_DIM), BF),
        jax.ShapeDtypeStruct((SUMM, NZ * HEAD_DIM), BF),
    ]
    scratch = [
        pltpu.SMEM((2 * NX * NY,), F32),
        pltpu.VMEM((SEG, GROUP * HEAD_DIM), BF),
        pltpu.VMEM((SEG, HEAD_DIM), BF),
        pltpu.VMEM((SEG, HEAD_DIM), BF),
        pltpu.VMEM((SEG, GROUP * HEAD_DIM), BF),
        pltpu.VMEM((2, 2 * NX) + column, BF),
        pltpu.VMEM((GROUP, width, SEG), F32),
        pltpu.VMEM((GROUP, width, SEG), F32),
        pltpu.VMEM((width, GROUP * SEG), BF),
        pltpu.VMEM((GROUP * SEG, HEAD_DIM), BF),
        pltpu.VMEM((GROUP * SEG, HEAD_DIM), BF),
        pltpu.VMEM((HEAD_DIM, width), BF),
        pltpu.VMEM((GROUP, SEG, HEAD_DIM), BF),
        pltpu.VMEM((GROUP, 8, SEG), F32),
        pltpu.VMEM((GROUP, 1, SEG), F32),
        pltpu.VMEM((GROUP, 1, SEG), F32),
        pltpu.VMEM((2, NX) + column, BF),
        pltpu.VMEM((2, NX) + column, BF),
        pltpu.VMEM((NX,) + column, F32),
        pltpu.VMEM((2, NX) + column, BF),
        pltpu.VMEM((2, NX) + column, BF),
        pltpu.VMEM((2,) + column, F32),
        pltpu.VMEM((2,) + column, BF),
        pltpu.VMEM((2,) + column, BF),
        pltpu.VMEM((2, SEG, HEAD_DIM), BF),
        pltpu.VMEM((2, SUMM, HEAD_DIM), F32),
        pltpu.VMEM((2, SUMM, HEAD_DIM), BF),
    ]
    pairs = [(2, NY), (2, NX), (2, NX), (2, NX), (2, NX), (2, NY), (NZ,), (2, NZ)]
    scratch += [pltpu.SemaphoreType.DMA((8,)), pltpu.SemaphoreType.DMA((2,))]
    scratch += [pltpu.SemaphoreType.DMA(shape) for shape in pairs for _ in range(2)]
    raw = pl.pallas_call(
        kernel,
        out_shape=outs,
        in_specs=[smem, hbm, hbm, hbm, hbm],
        out_specs=[hbm, hbm, hbm],
        scratch_shapes=scratch,
        compiler_params=pltpu.CompilerParams(
            collective_id=0, has_side_effects=True, vmem_limit_bytes=60 * 2**20
        ),
        name="attention_backward",
    )(seg_order, queries, key_rows, value_rows, grad_out)
    return pl.pallas_call(
        place,
        out_shape=outs,
        in_specs=[pl.BlockSpec(memory_space=pltpu.VMEM)] * 3,
        out_specs=[hbm, hbm, hbm],
        scratch_shapes=[pltpu.SemaphoreType.DMA((3,))],
        name="place",
    )(*raw)


def solution(mesh):
    in_specs = (P("seg", "tp"), P("seg", "tp"), P("seg", "tp"), P("seg", "tp"), P())
    out_specs = (P(("seg", "tp"), None), P(("seg", "tp"), None), P(("seg", "tp"), None))
    return jax.shard_map(backward, mesh=mesh, in_specs=in_specs, out_specs=out_specs, check_vma=False)
```

time: 306 us -> 62.3 us (0.20)
  blocking collectives: 104 us -> 0 us
  waiting for transfers between devices: 77.9 us -> 0 us
  Pallas kernels: 0 us -> 61.3 us
  matrix products: 51.1 us -> 0 us
  starting transfers between devices: 28.4 us -> 0 us
  local copies, waits for them, and re-layouts: 24.4 us -> 0 us
  other arithmetic: 16.2 us -> 0 us
    all_gather x2 -> x0, blocking collectives: 104 us -> none  [the longest x1 53.7 us: local(): lax.all_gather(key_rows[seg_len - SUMM:], 'seg', axis=0, tiled=True)]
    all_to_all x5 -> x0, waiting for transfers between devices: 77.9 us -> none  [the longest x1 26.9 us: local(): lax.all_to_all(prior_dv.reshape(slots, SUMM, kv_count * HEAD_DIM), 'seg',...]
    pallas_call x0 -> x2, Pallas kernels: none -> 61.3 us  [the longest x1 59.4 us: backward(): pl.pallas_call(kernel, out_shape=outs, in_specs=[smem, hbm, hbm, hbm, hbm...]
    dot_general x20 -> x0, matrix products: 51.1 us -> none  [the longest x4 20.1 us: head_step(): lax.dot_general(probs_low, g_rows, contract_first, preferred_element_type...]
    all_to_all x5 -> x0, starting transfers between devices: 28.4 us -> none  [the longest x1 7.67 us: local(): lax.all_to_all(dq_all, 'tp', split_axis=0, concat_axis=1, tiled=True)]
    while x24 -> x0, local copies, waits for them, and re-layouts: 8.56 us -> none
    convert_element_type x4 -> x0, other arithmetic: 6 us -> none  [head_step(): grad_scores = (probs * (grad_probs - delta_rows)).astype(jnp.bfloat16)]
    another operation x5 -> x0, local copies, waits for them, and re-layouts: 5.34 us -> none  [the longest x1 1.54 us: local(): dv_stack[:, :seg_len].transpose(1, 0, 2)]
  transfers between devices with their start and end apart: 5 -> 0, of which waited for: 5 -> 0; matrix products, arithmetic and copies ran while one was open for 3% -> 0% of each run, Pallas kernels for 0% -> 0%
where the time goes in v2:
time: 62.3 us; the launch traced here: 62.1 us
  Pallas kernels  61.3 us (98%)
  between operations  0.8 us (1%)
    pallas_call x1, Pallas kernels, backward(): pl.pallas_call(kernel, out_shape=outs, in_specs=[smem, hbm, hbm, hbm, hbm...  59.4 us
    pallas_call x1, Pallas kernels, backward(): pl.pallas_call(place, out_shape=outs, in_specs=[pl.BlockSpec(memory_space...  1.93 us

profile of v2, /device:TPU:1, one launch (start us, length us, event | category | flops | bytes accessed | tf_op | source)
XLA Modules:
  0.0 62.1 jit_solution(9481141275484410952)
XLA Ops:
  0.6 59.4 %attention_backward.1 = (bf16[32,8192]{1,0:T(8,128)(2,1)}, bf16[32,1024]{1,0:T(8,128)(2,1)}, bf16[32,1024]{1,0:T(8,128)(2,1)}) custom-call(s32[64]{0:T(128)} %order_ref.1, bf16[256,1024]{1,0:T(8,128)(2,1)} %q_hbm.1, bf16[256,128]{1,0:T(8,128)(2,1)} %k_hbm.1, bf16[256,128]{1,0:T(8,128)(2,1)} %v_hbm.1, bf16[256,1024]{1,0:T(8,128)(2,1)} %g_hbm.1), custom_call_target="tpu_custom_call" | custom-call | tf_op jit(solution)/shard_map/attention_backward/pallas_call | solution.py:416
  60.0 1.9 %place.1 = (bf16[32,8192]{1,0:T(8,128)(2,1)}, bf16[32,1024]{1,0:T(8,128)(2,1)}, bf16[32,1024]{1,0:T(8,128)(2,1)}) custom-call(bf16[32,8192]{1,0:T(8,128)(2,1)} %get-tuple-element.6.a_ref, bf16[32,1024]{1,0:T(8,128)(2,1)} %get-tuple-element.7.b_ref, bf16[32,1024]{1,0:T(8,128)(2,1)} %get-tuple-element.8.c_ref), custom_call_target="tpu_custom_call" | custom-call | tf_op jit(solution)/shard_map/place/pallas_call | solution.py:427

commit v3 on v2

--- a/solution.py
+++ b/solution.py
@@ -47,8 +47,8 @@
 
 def kernel(
     order_ref, q_hbm, k_hbm, v_hbm, g_hbm, oq_ref, ok_ref, ov_ref,
-    bias, q_ref, k_ref, v_ref, g_ref, buf, s_ref, dp_ref, e_ref, qp_ref, gp_ref, kt_ref, dq_ref,
-    top_ref, inv_ref, delta_ref,
+    bias, q_ref, k_ref, v_ref, g_ref, buf, s_ref, dp_ref, e_ref, ds_ref, qs_ref, gs_ref, kt_ref, dq_ref,
+    top_ref, total_ref, delta_ref,
     sib_out, sib_in, parts, x_out, x_in, x_own, y_out, y_in, local, summ, final,
     in_sem, own_sem, gy_s, gy_r, gx_s, gx_r, gs_s, gs_r,
     rs_s, rs_r, rx_s, rx_r, ry_s, ry_r, q_s, q_r, z_s, z_r,
@@ -93,7 +93,7 @@
     for copy in fetch:
         copy.start()
     barrier = pltpu.get_barrier_semaphore()
-    peers = [y_dev(r) for r in range(1, NY)] + [x_dev(r) for r in range(1, NX)]
+    peers = [y_dev(r) for r in FAR_FIRST] + [x_dev(r) for r in range(1, NX)]
     peers += [sibling] + [z_dev(r) for r in range(1, NZ)]
     for dev in peers:
         pl.semaphore_signal(barrier, inc=1, device_id=dev, device_id_type=MESH)
@@ -148,8 +148,9 @@
             return (k_ref if t == KEYS else v_ref)[...]
         return buf[t, block_of(slot)].reshape(SEG, HEAD_DIM)
 
-    def scores(slot):
+    def absorb(slot):
         kc = fetched(KEYS, slot)
+        vc = fetched(VALUES, slot)
         rows = rows_of(slot)
         kt_ref[:, rows] = kc.T
         for h in range(GROUP):
@@ -162,9 +163,15 @@
                 key_pos = lax.broadcasted_iota(jnp.int32, (SEG, SEG), 0)
                 query_pos = lax.broadcasted_iota(jnp.int32, (SEG, SEG), 1)
                 s = jnp.where(key_pos <= query_pos, s, HIDDEN)
-            s_ref[h, rows, :] = s
-            top = fold(s, jnp.max)
-            top_ref[h] = jnp.maximum(top_ref[h], top) if slot else top
+            s_ref[h] = s
+            top_ref[slot, h : h + 1] = jnp.max(fold(s, jnp.max), 0, keepdims=True)
+        for h in range(GROUP):
+            e = jnp.exp2(s_ref[h] - top_ref[slot, h : h + 1])
+            dp = dot_t(vc, g_ref[:, h * HEAD_DIM : (h + 1) * HEAD_DIM])
+            total_ref[slot, h : h + 1] = jnp.sum(fold(e, jnp.sum), 0, keepdims=True)
+            delta_ref[slot, h : h + 1] = jnp.sum(fold(e * dp, jnp.sum), 0, keepdims=True)
+            e_ref[rows, h * SEG : (h + 1) * SEG] = e.astype(BF)
+            dp_ref[h, rows, :] = dp
 
     def mask_terms():
         own = order_ref[seg]
@@ -175,69 +182,49 @@
     mask_terms()
     for copy in fetch[2:]:
         copy.wait()
-    scores(0)
+    for h in range(GROUP):
+        qs_ref[rows_of(h), :] = q_ref[:, h * HEAD_DIM : (h + 1) * HEAD_DIM]
+        gs_ref[rows_of(h), :] = g_ref[:, h * HEAD_DIM : (h + 1) * HEAD_DIM]
+    absorb(0)
     gather_y(KEYS)
-    scores(1)
+    gather_y(VALUES)
+    absorb(1)
     gs[KEYS, 0].wait_recv()
-    scores(2)
-    gather_y(VALUES)
+    gs[VALUES, 0].wait_recv()
+    absorb(2)
     for d in (3, 1, 2):
         gather_x(KEYS, d)
-    scores(7)
-    scores(3)
-    scores(5)
+    for d in (3, 1, 2):
+        gather_x(VALUES, d)
+        absorb(1 + 2 * d)
     for d in (3, 1, 2):
         gs[KEYS, d].wait_recv()
-    scores(8)
-    scores(4)
-    scores(6)
-
-    def weigh(h):
-        cols = aligned(h, HEAD_DIM)
-        wide = aligned(h, SEG)
-        top = jnp.max(top_ref[h], 0, keepdims=True)
-        total = jnp.zeros((8, SEG), F32)
-        for slot in range(CHUNKS):
-            rows = rows_of(slot)
-            e = jnp.exp2(s_ref[h, rows, :] - top)
-            total = total + fold(e, jnp.sum)
-            e_ref[rows, wide] = e.astype(BF)
-        inv = 1.0 / jnp.sum(total, 0, keepdims=True)
-        inv_ref[h] = inv
-        inv_rows = jnp.broadcast_to(inv, (HEAD_DIM, SEG)).T
-        qp_ref[wide, :] = (q_ref[:, cols].astype(F32) * (inv_rows * SCALE)).astype(BF)
-        gp_ref[wide, :] = (g_ref[:, cols].astype(F32) * inv_rows).astype(BF)
-
-    def weigh_pair(i, carry):
-        weigh(2 * i)
-        weigh(2 * i + 1)
-        return carry
-
-    lax.fori_loop(0, GROUP // 2, weigh_pair, 0)
-
-    def weigh_products(h):
-        cols = aligned(h, HEAD_DIM)
-        wide = aligned(h, SEG)
-        gh = g_ref[:, cols]
-        delta = jnp.zeros((8, SEG), F32)
-        for slot in range(CHUNKS):
-            rows = rows_of(slot)
-            dp = dot_t(fetched(VALUES, slot), gh)
-            delta = delta + fold(e_ref[rows, wide].astype(F32) * dp, jnp.sum)
-            dp_ref[h, rows, :] = dp
-        delta_ref[h] = jnp.sum(delta, 0, keepdims=True) * inv_ref[h]
-
-    def products_pair(i, carry):
-        weigh_products(2 * i)
-        weigh_products(2 * i + 1)
-        return carry
+        gs[VALUES, d].wait_recv()
+        absorb(2 + 2 * d)
+
+    top = top_ref[0]
+    for slot in range(1, CHUNKS):
+        top = jnp.maximum(top, top_ref[slot])
+    total = jnp.zeros((GROUP, SEG), F32)
+    delta = jnp.zeros((GROUP, SEG), F32)
+    for slot in range(CHUNKS):
+        factor = jnp.exp2(top_ref[slot] - top)
+        top_ref[slot] = factor
+        total = total + factor * total_ref[slot]
+        delta = delta + factor * delta_ref[slot]
+    inv = 1.0 / total
+    for slot in range(CHUNKS):
+        top_ref[slot] = top_ref[slot] * inv
+    delta_ref[0] = delta * inv
 
     my_cols = aligned(z, HEAD_DIM)
     my_rows = pl.ds(z * SUMM, SUMM)
     outs = (ok_ref, ov_ref)
 
     def terms(t, slot):
-        return dot(e_ref[rows_of(slot), :], (qp_ref if t == KEYS else gp_ref)[...])
+        if t == KEYS:
+            return dot(ds_ref[rows_of(slot), :], qs_ref[...]) * SCALE
+        return dot(e_ref[rows_of(slot), :], gs_ref[...])
 
     rs, rx, ry = {}, {}, {}
 
@@ -247,29 +234,40 @@
     def early(t, r):
         return z_copy(t, r, local.at[t, pl.ds(lax.rem(z + r, NZ) * SUMM, SUMM), :])
 
-    def score_grads(slot):
+    def normalise(slot):
         rows = rows_of(slot)
         for h in range(GROUP):
             wide = slice(h * SEG, (h + 1) * SEG)
-            e_ref[rows, wide] = (
-                e_ref[rows, wide].astype(F32) * (dp_ref[h, rows, :] - delta_ref[h])
-            ).astype(BF)
+            p = e_ref[rows, wide].astype(F32) * top_ref[slot, h : h + 1]
+            e_ref[rows, wide] = p.astype(BF)
+            ds_ref[rows, wide] = (p * (dp_ref[h, rows, :] - delta_ref[0, h : h + 1])).astype(BF)
 
     def reduce_x(t):
-        for d in (2, 1, 3, 0):
-            sib_out[t, d] = split(terms(t, 2 + 2 * d)).astype(BF)
-        for d in (2, 1, 3, 0):
-            rs[t, d] = go(remote(sib_out.at[t, d], sib_in.at[t, d], rs_s.at[t, d], rs_r.at[t, d], sibling))
-        for d in (2, 1, 3, 0):
-            parts[d] = split(terms(t, 1 + 2 * d))
-        for d in (2, 1, 3, 0):
-            rs[t, d].wait_recv()
-            part = parts[d] + sib_in[t, d].astype(F32)
-            if d:
-                x_out[t, d] = part.astype(BF)
-                rx[t, d] = go(remote(x_out.at[t, d], x_in.at[t, d], rx_s.at[t, d], rx_r.at[t, d], x_dev(d)))
-            else:
-                x_own[t] = part
+        def give(columns):
+            for d in columns:
+                sib_out[t, d] = split(terms(t, 2 + 2 * d)).astype(BF)
+            for d in columns:
+                rs[t, d] = go(remote(sib_out.at[t, d], sib_in.at[t, d], rs_s.at[t, d], rs_r.at[t, d], sibling))
+
+        def take(columns):
+            for d in columns:
+                parts[d] = split(terms(t, 1 + 2 * d))
+            for d in columns:
+                rs[t, d].wait_recv()
+                part = parts[d] + sib_in[t, d].astype(F32)
+                if d:
+                    x_out[t, d] = part.astype(BF)
+                    rx[t, d] = go(
+                        remote(x_out.at[t, d], x_in.at[t, d], rx_s.at[t, d], rx_r.at[t, d], x_dev(d))
+                    )
+                else:
+                    x_own[t] = part
+
+        give((2,))
+        give((1, 3, 0))
+        take((2,))
+        take((1, 3))
+        take((0,))
         part = terms(t, 0)
         local[t] = part.astype(BF)
         summ[t] = part[SEG - SUMM :]
@@ -316,26 +314,21 @@
 
     def query_grads(first):
         for h in (first, first + 1):
-            acc = dot(kt_ref[...], e_ref[:, h * SEG : (h + 1) * SEG])
-            dq_ref[h] = (acc * (inv_ref[h] * SCALE)).T.astype(BF)
+            acc = dot(kt_ref[...], ds_ref[:, h * SEG : (h + 1) * SEG])
+            dq_ref[h] = (acc * SCALE).T.astype(BF)
         for h in (first, first + 1):
             for r in FAR_FIRST:
                 to = pl.ds(lax.rem(z + r, NZ) * SUMM, SUMM)
                 remote(dq_ref.at[h, to, :], oq_ref.at[:, dq_cols(h)], q_s.at[r], q_r.at[r], z_dev(r)).start()
 
-    for d in (3, 1, 2):
-        gather_x(VALUES, d)
+    for slot in range(CHUNKS):
+        normalise(slot)
+    query_grads(0)
     reduce_x(VALUES)
-    for d in range(NX):
-        gs[VALUES, d].wait_recv()
-    lax.fori_loop(0, GROUP // 2, products_pair, 0)
-    for slot in range(CHUNKS):
-        score_grads(slot)
-    query_grads(0)
+    query_grads(2)
+    reduce_x(KEYS)
+    query_grads(4)
     reduce_y(VALUES)
-    reduce_x(KEYS)
-    query_grads(2)
-    query_grads(4)
     query_grads(6)
     own_dq = [
         pltpu.make_async_copy(dq_ref.at[h, my_rows, :], oq_ref.at[:, dq_cols(h)], in_sem.at[h])
@@ -343,8 +336,8 @@
     ]
     for copy in own_dq:
         copy.start()
+    reduce_y(KEYS)
     reduce_end(VALUES)
-    reduce_y(KEYS)
     reduce_end(KEYS)
 
     for copy in own_dq:
@@ -360,14 +353,18 @@
         copy.wait_send()
 
 
-def place(a_ref, b_ref, c_ref, oa_ref, ob_ref, oc_ref, sem):
-    copies = [
-        pltpu.make_async_copy(src, dst, sem.at[i])
-        for i, (src, dst) in enumerate(((a_ref, oa_ref), (b_ref, ob_ref), (c_ref, oc_ref)))
-    ]
-    for copy in copies:
+def place(a_ref, b_ref, c_ref, oa_ref, ob_ref, oc_ref, mid, get_sem, put_sem):
+    width = mid.shape[2]
+    pieces = [(a_ref.at[:, pl.ds(i * width, width)], oa_ref.at[:, pl.ds(i * width, width)]) for i in range(8)]
+    pieces += [(b_ref, ob_ref), (c_ref, oc_ref)]
+    gets = [pltpu.make_async_copy(src, mid.at[i], get_sem.at[i]) for i, (src, _) in enumerate(pieces)]
+    puts = [pltpu.make_async_copy(mid.at[i], dst, put_sem.at[i]) for i, (_, dst) in enumerate(pieces)]
+    for copy in gets:
         copy.start()
-    for copy in copies:
+    for get, put in zip(gets, puts):
+        get.wait()
+        put.start()
+    for copy in puts:
         copy.wait()
 
 
@@ -388,16 +385,17 @@
         pltpu.VMEM((SEG, HEAD_DIM), BF),
         pltpu.VMEM((SEG, GROUP * HEAD_DIM), BF),
         pltpu.VMEM((2, 2 * NX) + column, BF),
+        pltpu.VMEM((GROUP, SEG, SEG), F32),
         pltpu.VMEM((GROUP, width, SEG), F32),
-        pltpu.VMEM((GROUP, width, SEG), F32),
+        pltpu.VMEM((width, GROUP * SEG), BF),
         pltpu.VMEM((width, GROUP * SEG), BF),
         pltpu.VMEM((GROUP * SEG, HEAD_DIM), BF),
         pltpu.VMEM((GROUP * SEG, HEAD_DIM), BF),
         pltpu.VMEM((HEAD_DIM, width), BF),
         pltpu.VMEM((GROUP, SEG, HEAD_DIM), BF),
-        pltpu.VMEM((GROUP, 8, SEG), F32),
-        pltpu.VMEM((GROUP, 1, SEG), F32),
-        pltpu.VMEM((GROUP, 1, SEG), F32),
+        pltpu.VMEM((CHUNKS, GROUP, SEG), F32),
+        pltpu.VMEM((CHUNKS, GROUP, SEG), F32),
+        pltpu.VMEM((CHUNKS, GROUP, SEG), F32),
         pltpu.VMEM((2, NX) + column, BF),
         pltpu.VMEM((2, NX) + column, BF),
         pltpu.VMEM((NX,) + column, F32),
@@ -420,16 +418,21 @@
         out_specs=[hbm, hbm, hbm],
         scratch_shapes=scratch,
         compiler_params=pltpu.CompilerParams(
-            collective_id=0, has_side_effects=True, vmem_limit_bytes=60 * 2**20
+            collective_id=0, has_side_effects=True, vmem_limit_bytes=62 * 2**20
         ),
         name="attention_backward",
     )(seg_order, queries, key_rows, value_rows, grad_out)
     return pl.pallas_call(
         place,
         out_shape=outs,
-        in_specs=[pl.BlockSpec(memory_space=pltpu.VMEM)] * 3,
+        in_specs=[hbm, hbm, hbm],
         out_specs=[hbm, hbm, hbm],
-        scratch_shapes=[pltpu.SemaphoreType.DMA((3,))],
+        scratch_shapes=[
+            pltpu.VMEM((10, SUMM, NZ * HEAD_DIM), BF),
+            pltpu.SemaphoreType.DMA((10,)),
+            pltpu.SemaphoreType.DMA((10,)),
+        ],
+        compiler_params=pltpu.CompilerParams(vmem_limit_bytes=62 * 2**20),
         name="place",
     )(*raw)
 

time: 62.3 us -> 59.1 us (0.949)
  Pallas kernels: 61.3 us -> 58.1 us
    pallas_call x1, Pallas kernels: 59.4 us -> 56.1 us  [backward(): pl.pallas_call(kernel, out_shape=outs, in_specs=[smem, hbm, hbm, hbm, hbm...]
where the time goes in v3:
time: 59.1 us; the launch traced here: 58.9 us
  Pallas kernels  58.1 us (98%)
  between operations  0.8 us (1%)
    pallas_call x1, Pallas kernels, backward(): pl.pallas_call(kernel, out_shape=outs, in_specs=[smem, hbm, hbm, hbm, hbm...  56.1 us
    pallas_call x1, Pallas kernels, backward(): pl.pallas_call(place, out_shape=outs, in_specs=[hbm, hbm, hbm], out_specs...  1.93 us

profile of v3, /device:TPU:1, one launch (start us, length us, event | category | flops | bytes accessed | tf_op | source)
XLA Modules:
  0.0 58.9 jit_solution(6326187707686000146)
XLA Ops:
  0.6 56.1 %attention_backward.1 = (bf16[32,8192]{1,0:T(8,128)(2,1)}, bf16[32,1024]{1,0:T(8,128)(2,1)}, bf16[32,1024]{1,0:T(8,128)(2,1)}) custom-call(s32[64]{0:T(128)} %order_ref.1, bf16[256,1024]{1,0:T(8,128)(2,1)} %q_hbm.1, bf16[256,128]{1,0:T(8,128)(2,1)} %k_hbm.1, bf16[256,128]{1,0:T(8,128)(2,1)} %v_hbm.1, bf16[256,1024]{1,0:T(8,128)(2,1)} %g_hbm.1), custom_call_target="tpu_custom_call" | custom-call | tf_op jit(solution)/shard_map/attention_backward/pallas_call | solution.py:414
  56.8 1.9 %place.1 = (bf16[32,8192]{1,0:T(8,128)(2,1)}, bf16[32,1024]{1,0:T(8,128)(2,1)}, bf16[32,1024]{1,0:T(8,128)(2,1)}) custom-call(bf16[32,8192]{1,0:T(8,128)(2,1)} %get-tuple-element.6.a_ref, bf16[32,1024]{1,0:T(8,128)(2,1)} %get-tuple-element.7.b_ref, bf16[32,1024]{1,0:T(8,128)(2,1)} %get-tuple-element.8.c_ref), custom_call_target="tpu_custom_call" | custom-call | tf_op jit(solution)/shard_map/place/pallas_call | solution.py:425

commit v4 on v3

--- a/solution.py
+++ b/solution.py
@@ -116,7 +116,7 @@
             )
 
     def spread_x(t, block):
-        for r in (2, 1, 3):
+        for r in (1, 3):
             remote(block, block, gx_s.at[t, r], gx_r.at[t, r], x_dev(r)).start()
 
     def column_x(t, r):
@@ -128,17 +128,17 @@
         gs[t, d] = go(remote(block, block, gs_s.at[t, d], gs_r.at[t, d], sibling))
 
     def gather_y(t):
-        spread_x(t, buf.at[t, mine, y])
         for r in (1, 7, 2, 6, 3, 5, 4):
             gy[t, r].wait_recv()
             spread_x(t, buf.at[t, mine, lax.rem(y + NY - r, NY)])
         to_sibling(t, 0)
-        for r in range(1, NX):
-            sends.append(column_x(t, r))
 
     def gather_x(t, d):
         column_x(t, NX - d).wait_recv()
         to_sibling(t, d)
+
+    for t in (KEYS, VALUES):
+        spread_x(t, buf.at[t, mine, y])
 
     def block_of(slot):
         return column((slot - 1) // 2, core if slot % 2 else 1 - core)
@@ -188,19 +188,31 @@
     absorb(0)
     gather_y(KEYS)
     gather_y(VALUES)
+    for t in (KEYS, VALUES):
+        column_x(t, 2).start()
+        for r in range(1, NX):
+            sends.append(column_x(t, r))
     absorb(1)
     gs[KEYS, 0].wait_recv()
     gs[VALUES, 0].wait_recv()
     absorb(2)
-    for d in (3, 1, 2):
-        gather_x(KEYS, d)
-    for d in (3, 1, 2):
-        gather_x(VALUES, d)
-        absorb(1 + 2 * d)
-    for d in (3, 1, 2):
+    for t in (KEYS, VALUES):
+        for d in (3, 1):
+            gather_x(t, d)
+
+    def absorb_sibling(d):
         gs[KEYS, d].wait_recv()
         gs[VALUES, d].wait_recv()
         absorb(2 + 2 * d)
+
+    absorb(7)
+    absorb(3)
+    absorb_sibling(3)
+    for t in (KEYS, VALUES):
+        gather_x(t, 2)
+    absorb_sibling(1)
+    absorb(5)
+    absorb_sibling(2)
 
     top = top_ref[0]
     for slot in range(1, CHUNKS):
@@ -242,33 +254,34 @@
             e_ref[rows, wide] = p.astype(BF)
             ds_ref[rows, wide] = (p * (dp_ref[h, rows, :] - delta_ref[0, h : h + 1])).astype(BF)
 
+    def give(t, columns):
+        for d in columns:
+            sib_out[t, d] = split(terms(t, 2 + 2 * d)).astype(BF)
+        for d in columns:
+            rs[t, d] = go(remote(sib_out.at[t, d], sib_in.at[t, d], rs_s.at[t, d], rs_r.at[t, d], sibling))
+
+    def take(t, columns):
+        for d in columns:
+            parts[d] = split(terms(t, 1 + 2 * d))
+        for d in columns:
+            rs[t, d].wait_recv()
+            part = parts[d] + sib_in[t, d].astype(F32)
+            if d:
+                x_out[t, d] = part.astype(BF)
+                rx[t, d] = go(remote(x_out.at[t, d], x_in.at[t, d], rx_s.at[t, d], rx_r.at[t, d], x_dev(d)))
+            else:
+                x_own[t] = part
+
     def reduce_x(t):
-        def give(columns):
-            for d in columns:
-                sib_out[t, d] = split(terms(t, 2 + 2 * d)).astype(BF)
-            for d in columns:
-                rs[t, d] = go(remote(sib_out.at[t, d], sib_in.at[t, d], rs_s.at[t, d], rs_r.at[t, d], sibling))
-
-        def take(columns):
-            for d in columns:
-                parts[d] = split(terms(t, 1 + 2 * d))
-            for d in columns:
-                rs[t, d].wait_recv()
-                part = parts[d] + sib_in[t, d].astype(F32)
-                if d:
-                    x_out[t, d] = part.astype(BF)
-                    rx[t, d] = go(
-                        remote(x_out.at[t, d], x_in.at[t, d], rx_s.at[t, d], rx_r.at[t, d], x_dev(d))
-                    )
-                else:
-                    x_own[t] = part
-
-        give((2,))
-        give((1, 3, 0))
-        take((2,))
-        take((1, 3))
-        take((0,))
+        give(t, (2,))
+        give(t, (1, 3))
+        take(t, (2,))
+        take(t, (1, 3))
+
+    def reduce_own(t):
+        give(t, (0,))
         part = terms(t, 0)
+        take(t, (0,))
         local[t] = part.astype(BF)
         summ[t] = part[SEG - SUMM :]
         for r in range(1, NZ):
@@ -324,19 +337,21 @@
     for slot in range(CHUNKS):
         normalise(slot)
     query_grads(0)
+    query_grads(2)
     reduce_x(VALUES)
-    query_grads(2)
+    query_grads(4)
     reduce_x(KEYS)
-    query_grads(4)
+    query_grads(6)
+    reduce_own(VALUES)
+    reduce_own(KEYS)
     reduce_y(VALUES)
-    query_grads(6)
+    reduce_y(KEYS)
     own_dq = [
         pltpu.make_async_copy(dq_ref.at[h, my_rows, :], oq_ref.at[:, dq_cols(h)], in_sem.at[h])
         for h in range(GROUP)
     ]
     for copy in own_dq:
         copy.start()
-    reduce_y(KEYS)
     reduce_end(VALUES)
     reduce_end(KEYS)
 

time: 59.1 us -> 56.2 us (0.951)
  Pallas kernels: 58.1 us -> 55.2 us
    pallas_call x1, Pallas kernels: 56.1 us -> 53.3 us  [backward(): pl.pallas_call(kernel, out_shape=outs, in_specs=[smem, hbm, hbm, hbm, hbm...]
where the time goes in v4:
time: 56.2 us; the launch traced here: 56 us
  Pallas kernels  55.2 us (98%)
  between operations  0.8 us (1%)
    pallas_call x1, Pallas kernels, backward(): pl.pallas_call(kernel, out_shape=outs, in_specs=[smem, hbm, hbm, hbm, hbm...  53.3 us
    pallas_call x1, Pallas kernels, backward(): pl.pallas_call(place, out_shape=outs, in_specs=[hbm, hbm, hbm], out_specs...  1.93 us

profile of v4, /device:TPU:1, one launch (start us, length us, event | category | flops | bytes accessed | tf_op | source)
XLA Modules:
  0.0 56.0 jit_solution(12418495496760137316)
XLA Ops:
  0.6 53.3 %attention_backward.1 = (bf16[32,8192]{1,0:T(8,128)(2,1)}, bf16[32,1024]{1,0:T(8,128)(2,1)}, bf16[32,1024]{1,0:T(8,128)(2,1)}) custom-call(s32[64]{0:T(128)} %order_ref.1, bf16[256,1024]{1,0:T(8,128)(2,1)} %q_hbm.1, bf16[256,128]{1,0:T(8,128)(2,1)} %k_hbm.1, bf16[256,128]{1,0:T(8,128)(2,1)} %v_hbm.1, bf16[256,1024]{1,0:T(8,128)(2,1)} %g_hbm.1), custom_call_target="tpu_custom_call" | custom-call | tf_op jit(solution)/shard_map/attention_backward/pallas_call | solution.py:429
  53.9 1.9 %place.1 = (bf16[32,8192]{1,0:T(8,128)(2,1)}, bf16[32,1024]{1,0:T(8,128)(2,1)}, bf16[32,1024]{1,0:T(8,128)(2,1)}) custom-call(bf16[32,8192]{1,0:T(8,128)(2,1)} %get-tuple-element.6.a_ref, bf16[32,1024]{1,0:T(8,128)(2,1)} %get-tuple-element.7.b_ref, bf16[32,1024]{1,0:T(8,128)(2,1)} %get-tuple-element.8.c_ref), custom_call_target="tpu_custom_call" | custom-call | tf_op jit(solution)/shard_map/place/pallas_call | solution.py:440

commit v5 on v4

--- a/solution.py
+++ b/solution.py
@@ -343,8 +343,8 @@
     reduce_x(KEYS)
     query_grads(6)
     reduce_own(VALUES)
+    reduce_y(VALUES)
     reduce_own(KEYS)
-    reduce_y(VALUES)
     reduce_y(KEYS)
     own_dq = [
         pltpu.make_async_copy(dq_ref.at[h, my_rows, :], oq_ref.at[:, dq_cols(h)], in_sem.at[h])

time: 56.2 us -> 56.2 us (level)
  no operation moved by 1% of the time
where the time goes in v5:
time: 56.2 us; the launch traced here: 56 us
  Pallas kernels  55.2 us (98%)
  between operations  0.8 us (1%)
    pallas_call x1, Pallas kernels, backward(): pl.pallas_call(kernel, out_shape=outs, in_specs=[smem, hbm, hbm, hbm, hbm...  53.3 us
    pallas_call x1, Pallas kernels, backward(): pl.pallas_call(place, out_shape=outs, in_specs=[hbm, hbm, hbm], out_specs...  1.93 us

profile of v5, /device:TPU:1, one launch (start us, length us, event | category | flops | bytes accessed | tf_op | source)
XLA Modules:
  0.0 56.0 jit_solution(6406549752845985989)
XLA Ops:
  0.6 53.3 %attention_backward.1 = (bf16[32,8192]{1,0:T(8,128)(2,1)}, bf16[32,1024]{1,0:T(8,128)(2,1)}, bf16[32,1024]{1,0:T(8,128)(2,1)}) custom-call(s32[64]{0:T(128)} %order_ref.1, bf16[256,1024]{1,0:T(8,128)(2,1)} %q_hbm.1, bf16[256,128]{1,0:T(8,128)(2,1)} %k_hbm.1, bf16[256,128]{1,0:T(8,128)(2,1)} %v_hbm.1, bf16[256,1024]{1,0:T(8,128)(2,1)} %g_hbm.1), custom_call_target="tpu_custom_call" | custom-call | tf_op jit(solution)/shard_map/attention_backward/pallas_call | solution.py:429
  53.9 1.9 %place.1 = (bf16[32,8192]{1,0:T(8,128)(2,1)}, bf16[32,1024]{1,0:T(8,128)(2,1)}, bf16[32,1024]{1,0:T(8,128)(2,1)}) custom-call(bf16[32,8192]{1,0:T(8,128)(2,1)} %get-tuple-element.6.a_ref, bf16[32,1024]{1,0:T(8,128)(2,1)} %get-tuple-element.7.b_ref, bf16[32,1024]{1,0:T(8,128)(2,1)} %get-tuple-element.8.c_ref), custom_call_target="tpu_custom_call" | custom-call | tf_op jit(solution)/shard_map/place/pallas_call | solution.py:440
